TPU v7x, 32 devices: a whole 2x2x4 slice. The times are simulated.
32 devices in a mesh: groups: 2 (over y), dp: 4 (over z), shard: 4 (over x, core).
Axes of the slice: x: 2, y: 2, z: 4, core: 2. Of those that a mesh axis runs over, the one named last changes fastest.
Arguments:
- acts: bfloat16 [256, 4096], P(('groups', 'dp'), 'shard'), parts along dimension 0, may hold values from -6 to 6
- grads: bfloat16 [256, 16384], P(('groups', 'dp')), parts along dimension 0, may hold values from -6 to 6
- lengths: int32 [16], P(('groups', 'dp')), parts along dimension 0, may hold values from 1 to 16, 96 in all
- act_basis: bfloat16 [16, 256, 256], P('shard'), may hold values from -0.375 to 0.375
- grad_basis: bfloat16 [64, 256, 256], P('dp'), may hold values from -0.375 to 0.375
- correction: bfloat16 [4096, 16384], P('shard', 'dp'), may hold values from 0.0099487305 to 3
- val_grads: bfloat16 [6, 4096, 16384], P(None, 'shard', 'dp'), may hold values from -9.1552734e-05 to 9.1552734e-05
Outputs:
- scores: float32 [16, 6], P(('groups', 'dp')), parts along dimension 0
- act_cov: float32 [32, 256, 256], P(('groups', 'shard'), 'dp'), parts along dimension 0
- grad_cov: float32 [128, 256, 256], P(('groups', 'dp'), 'shard'), parts along dimension 0
There are 2 independent parts, one for each index of `groups`. A program takes and returns all parts, laid end to end along the dimension named above; an argument that names none is the same for every part. Nothing has to cross between parts.
Inputs may be any that keep to these rules, and one draw needn't show every extreme that they name: lengths[s] counts the real tokens at the start of sequence s, the rest of its 16 slots being padding; the lengths of a pool add up to 96.
All inputs are finite; a program needn't handle non-finite values. No bound on the sum of `lengths` on one device may be relied on, other than what follows from the above.
Results may differ from a plain program's by a relative error of at most 0.008.
Values may be sent and summed in bfloat16 or wider, within the bound.
A program may use at most 192 MiB of HBM per device.

v0:
```python
import jax
import jax.numpy as jnp
from jax import lax
from jax.sharding import PartitionSpec as P

damping = 0.1


def rotate_blocks(row_data, eigen_basis):
    row_count = row_data.shape[0]
    block_count = eigen_basis.shape[0]
    block_width = eigen_basis.shape[1]
    blocked = row_data.reshape(row_count, block_count, block_width)
    rotated = jnp.einsum("tbi,bij->tbj", blocked, eigen_basis, preferred_element_type=jnp.float32)
    return rotated.reshape(row_count, block_count * block_width).astype(jnp.bfloat16)


def block_products(left_rows, right_rows):
    return jnp.einsum("tbi,tbj->bij", left_rows, right_rows, preferred_element_type=jnp.float32)


def local(acts, grads, lengths, act_basis, grad_basis, correction, val_grads):
    n_data = lax.axis_size("dp")
    n_shard = lax.axis_size("shard")
    tok_dev = acts.shape[0]
    seq_len = tok_dev // lengths.shape[0]
    total_tokens = tok_dev * n_data
    block_width = act_basis.shape[1]
    queries = val_grads.shape[0]
    position = jnp.arange(tok_dev, dtype=jnp.int32) % seq_len
    token_keep = (position < jnp.repeat(lengths, seq_len)).astype(jnp.bfloat16)[:, None]
    act_masked = acts * token_keep
    grad_masked = grads * token_keep
    act_turned = rotate_blocks(act_masked, act_basis)
    act_blocks = act_masked.reshape(tok_dev, -1, block_width)
    act_cov = (
        lax.psum_scatter(
            block_products(act_blocks, act_blocks).astype(jnp.bfloat16),
            "dp",
            scatter_dimension=1,
            tiled=True,
        ).astype(jnp.float32)
        / total_tokens
    )
    grad_cols = lax.all_to_all(grad_masked, "dp", split_axis=1, concat_axis=0, tiled=True)
    grad_turned = rotate_blocks(grad_cols, grad_basis)
    grad_blocks = grad_cols.reshape(total_tokens, -1, block_width)
    rows_each = block_width // n_shard
    own_rows = lax.dynamic_slice_in_dim(
        grad_blocks, lax.axis_index("shard") * rows_each, rows_each, 2
    )
    grad_cov = block_products(own_rows, grad_blocks) / total_tokens
    precond = (val_grads.astype(jnp.float32) / (correction.astype(jnp.float32) + damping)).astype(
        jnp.bfloat16
    )
    arrived = lax.all_gather(act_turned, "dp", axis=0, tiled=True)
    row_count = arrived.shape[0]
    mixed_terms = jnp.einsum(
        "tj,qij->tqi", grad_turned, precond, preferred_element_type=jnp.float32
    )
    token_scores = jnp.sum(mixed_terms * arrived.astype(jnp.float32)[:, None, :], axis=2)
    seq_scores = token_scores.reshape(row_count // seq_len, seq_len, queries).sum(axis=1)
    everything = lax.psum(seq_scores, ("dp", "shard"))
    seq_dev = lengths.shape[0]
    scores = lax.dynamic_slice_in_dim(everything, lax.axis_index("dp") * seq_dev, seq_dev, 0)
    return (scores, act_cov, grad_cov)


def solution(mesh):
    in_specs = (
        P(("groups", "dp"), "shard"),
        P(("groups", "dp"), None),
        P(("groups", "dp")),
        P("shard", None, None),
        P("dp", None, None),
        P("shard", "dp"),
        P(None, "shard", "dp"),
    )
    out_specs = (
        P(("groups", "dp"), None),
        P(("groups", "shard"), "dp", None),
        P(("groups", "dp"), "shard", None),
    )
    return jax.shard_map(local, mesh=mesh, in_specs=in_specs, out_specs=out_specs, check_vma=False)
```

profile of v0, /device:TPU:0, one launch (start us, length us, event | category | flops | bytes accessed | tf_op | source)
XLA Modules:
  0.0 146.0 jit_solution(752487040727854954)
XLA Ops:
  7.2 0.0 copy-start
  7.2 0.9 broadcast_in_dim.2
  8.1 0.1 reshape.45
  8.1 1.4 broadcast_multiply_fusion
  9.5 1.1 copy.67
  10.6 6.3 %all-to-all-start = ((bf16[32,4,4096]{2,0,1:T(8,128)(2,1)}), bf16[32,4,4096]{2,0,1:T(8,128)(2,1)S(1)}, u32[]{:S(2)}, u32[]{:S(2)}) async-start(bf16[32,4,4096]{2,0,1:T(8,128)(2,1)} %bitcast.33), calls=%async_computation | async-start | bytes 2097152 | tf_op jit(solution)/shard_map/all_to_all | solution.py:45
  16.9 0.0 reduce-scatter.2.cloned.1.call-start
  16.9 0.9 broadcast_multiply_fusion.1
  17.8 1.1 convolution_convert_fusion.1
  19.0 0.0 reduce-scatter.2.cloned.1.call-update
  19.0 1.2 fusion.2
  20.2 38.5 %all_gather.3 = bf16[128,1024]{1,0:T(8,128)(2,1)S(1)} all-gather(bf16[32,1024]{1,0:T(8,128)(2,1)S(1)} %bitcast.37), channel_id=1, replica_groups=mesh['groups'=2,'dp'=4,'shard'=4] {'dp'}, dimensions={0}, use_global_device_ids=true | all-gather | bytes 327680 | tf_op jit(solution)/shard_map/all_gather | solution.py:56
  58.7 0.9 convert_element_type.53
  59.6 11.5 %convert_add_fusion = f32[1024,4096]{1,0:T(8,128)} fusion(bf16[1024,4096]{1,0:T(8,128)(2,1)} %param.12), kind=kLoop, calls=%fused_computation.2 | loop fusion | flops 8388608 | bytes 25165824 | tf_op jit(solution)/shard_map/add | solution.py:53
  71.0 0.0 reduce-scatter.2.cloned.1.call-done
  71.0 1.6 %convert_multiply_fusion = f32[4,64,256]{2,1,0:T(8,128)} fusion(bf16[4,64,256]{2,1,0:T(8,128)(2,1)} %reduce-scatter.2.cloned.1.call-done), kind=kLoop, calls=%fused_computation.15 | loop fusion | flops 131072 | bytes 393216 | tf_op jit(solution)/shard_map/div | solution.py:37
  72.7 0.0 all-to-all-done
  72.7 0.0 copy-start.2
  72.7 1.0 copy-done.2
  73.6 1.5 %copy.51 = bf16[16,8,16,256]{3,2,1,0:T(8,128)(2,1)S(1)} copy(bf16[16,8,16,256]{3,1,2,0:T(8,128)(2,1)} %bitcast.32) | data formatting | bytes 2097152
  75.1 0.0 copy-done
  75.1 1.5 %fusion.1 = bf16[128,16,256]{2,0,1:T(8,128)(2,1)} fusion(bf16[16,256,256]{2,1,0:T(8,128)(2,1)S(1)} %copy-done, bf16[128,16,256]{2,1,0:T(8,128)(2,1)S(1)} %bitcast.28), kind=kOutput, calls=%fused_computation.5 | convolution fusion | flops 268959744 | bytes 4194304 | tf_op jit(solution)/shard_map/tbi,bij->tbj/dot_general | solution.py:14
  76.7 2.3 %copy.36 = bf16[128,16,256]{0,2,1:T(8,128)(2,1)} copy(bf16[128,16,256]{2,0,1:T(8,128)(2,1)} %fusion.1) | data formatting | bytes 2097152 | tf_op jit(solution)/shard_map/convert_element_type | solution.py:15
  78.9 0.0 copy-start.1
  78.9 27.8 %multiply_reduce_fusion = f32[128,6]{0,1:T(8,128)S(1)} fusion(f32[128,1024]{1,0:T(8,128)} %convert_element_type.53, bf16[128,4096,1]{0,1,2:T(8,128)(2,1)} %bitcast.34, bf16[6,1024,4096]{2,1,0:T(8,128)(2,1)} %param.13, f32[1024,4096]{1,0:T(8,128)} %convert_add_fusion), kind=kOutput, calls=%fused_computation.3 | convolution fusion | flops 6519520256 | bytes 68684800 | tf_op jit(solution)/shard_map/tj,qij->tqi/dot_general | solution.py:58
  106.7 0.1 reshape.48
  106.8 0.1 reduce_sum.19
  106.9 29.8 %psum.7 = f32[8,6]{0,1:T(8,128)S(1)} all-reduce(f32[8,6]{0,1:T(8,128)S(1)} %reduce_sum.19), channel_id=1, replica_groups=mesh['groups'=2,'dp'=4,'shard'=4] {'dp','shard'}, use_global_device_ids=true, to_apply=%region_2.3 | all-reduce | flops 48 | bytes 384 | tf_op jit(solution)/shard_map/psum | solution.py:63
  136.6 0.1 constant_dynamic-slice_fusion.1
  136.7 0.7 copy.44
  137.4 0.2 constant_dynamic-slice_fusion
  137.6 1.6 %convolution_multiply_fusion = f32[16,64,256]{2,1,0:T(8,128)} fusion(bf16[128,16,256]{2,1,0:T(8,128)(2,1)S(1)} %bitcast.30, bf16[128,16,64]{2,1,0:T(8,128)(2,1)S(1)} %constant_dynamic-slice_fusion), kind=kOutput, calls=%fused_computation.6 | convolution fusion | flops 67371008 | bytes 2359296 | tf_op jit(solution)/shard_map/tbi,tbj->bij/dot_general | solution.py:19
  139.1 0.0 copy-done.1
  (2 shorter events, 0.0 us)
Async XLA Ops:
  7.2 68.0 %copy-start = (bf16[16,256,256]{2,1,0:T(8,128)(2,1)S(1)}, bf16[16,256,256]{2,1,0:T(8,128)(2,1)}, u32[]{:S(2)}) copy-start(bf16[16,256,256]{2,1,0:T(8,128)(2,1)} %param.11) | copy-start | bytes 6291460
  10.6 62.1 %all-to-all-start = ((bf16[32,4,4096]{2,0,1:T(8,128)(2,1)}), bf16[32,4,4096]{2,0,1:T(8,128)(2,1)S(1)}, u32[]{:S(2)}, u32[]{:S(2)}) async-start(bf16[32,4,4096]{2,0,1:T(8,128)(2,1)} %bitcast.33), calls=%async_computation | async-start | bytes 2097152 | tf_op jit(solution)/shard_map/all_to_all | solution.py:45
  16.9 54.1 %reduce-scatter.2.cloned.1.call-start = ((), (), s32[]{:S(2)}) async-start(), calls=%async_computation.2 | async-start | bytes 655360 | tf_op jit(solution)/shard_map/reduce_scatter | solution.py:37
  72.7 1.0 copy-start.2
  78.9 60.2 %copy-start.1 = (bf16[16,256,256]{2,1,0:T(8,128)(2,1)S(1)}, bf16[16,256,256]{2,1,0:T(8,128)(2,1)}, u32[]{:S(2)}) copy-start(bf16[16,256,256]{2,1,0:T(8,128)(2,1)} %param.11) | copy-start | bytes 6291460
Sparse Core Ops, SparseCore 0:
  20.0 29.7 reduce-scatter.1
where the time goes:
time: 146 us
  blocking collectives  68.2 us (47%)
  matrix products  33.2 us (23%)
  other arithmetic  16.3 us (11%)
  between operations  14.1 us (10%)
  local copies, waits for them, and re-layouts  7.77 us (5%)
  starting transfers between devices  6.32 us (4%)
    all_gather x1, blocking collectives, local(): arrived = lax.all_gather(act_turned, 'dp', axis=0, tiled=True)  38.5 us
    psum x1, blocking collectives, local(): everything = lax.psum(seq_scores, ('dp', 'shard'))  29.8 us
    dot_general x1, matrix products, local(): jnp.einsum('tj,qij->tqi', grad_turned, precond, preferred_element_type=jn...  27.8 us
    add x1, other arithmetic, local(): correction.astype(jnp.float32) + damping  11.5 us
    all_to_all x1, starting transfers between devices, local(): lax.all_to_all(grad_masked, 'dp', split_axis=1, concat_axis=0, tiled=True)  6.32 us
    unnamed x8, local copies, waits for them, and re-layouts  3.11 us
  transfers between devices with their start and end apart: 2, of which 0 were waited for; matrix products, arithmetic and copies ran while one was open for 12% of the time, Pallas kernels for 0%

commit v1 on v0

--- a/solution.py
+++ b/solution.py
@@ -1,9 +1,17 @@
+import functools
+
 import jax
 import jax.numpy as jnp
 from jax import lax
+from jax.experimental import pallas as pl
+from jax.experimental.pallas import tpu as pltpu
 from jax.sharding import PartitionSpec as P
 
 damping = 0.1
+MESH = pl.DeviceIdType.MESH
+MIB = 1 << 20
+VMEM_LIMIT = 62 * MIB
+STREAM_BYTES = 46 * MIB
 
 
 def rotate_blocks(row_data, eigen_basis):
@@ -19,7 +27,7 @@
     return jnp.einsum("tbi,tbj->bij", left_rows, right_rows, preferred_element_type=jnp.float32)
 
 
-def local(acts, grads, lengths, act_basis, grad_basis, correction, val_grads):
+def local_plain(acts, grads, lengths, act_basis, grad_basis, correction, val_grads):
     n_data = lax.axis_size("dp")
     n_shard = lax.axis_size("shard")
     tok_dev = acts.shape[0]
@@ -66,6 +74,341 @@
     return (scores, act_cov, grad_cov)
 
 
+def kernel(
+    n_dp, n_shard, chunk, slots, kstep,
+    len_ref, acts_ref, grads_ref, abasis_ref, gbasis_ref, corr_ref, val_ref,
+    scores_ref, acov_ref, gcov_ref,
+    gbuf, gsend, abuf, abasis, gbasis, g_t, a_t, turn, val_buf, corr_buf, acc, red_dp, red_sh,
+    own_sem, out_sem, act_sem, ab_sem, gb_sem, val_sem, corr_sem,
+    gsend_sem, grecv_sem, asend_sem, arecv_sem, fx_sem, fc_sem, fr_sem,
+    rds_sem, rdr_sem, rss_sem, rsr_sem,
+):
+    d = lax.axis_index("dp")
+    s = lax.axis_index("shard")
+    tok = acts_ref.shape[0]
+    n_seq = len_ref.shape[0]
+    seq_len = tok // n_seq
+    tokens = tok * n_dp
+    blk = abasis_ref.shape[1]
+    a_blocks = abasis_ref.shape[0]
+    g_blocks = gbasis_ref.shape[0]
+    queries, rows, cols = val_ref.shape
+    part = cols // n_shard
+    part_blocks = part // blk
+    chunks = rows // chunk
+
+    other_core = s + 1 - 2 * lax.rem(s, 2)
+    other_chip = lax.rem(s + 2, 4)
+    across = other_core + 2 - 4 * (other_core // 2)
+    peers = [lax.rem(d + k, n_dp) for k in range(1, n_dp)]
+
+    def own_copy(j):
+        start = pl.multiple_of(d * cols + j * part, part)
+        return pltpu.make_async_copy(grads_ref.at[:, pl.ds(start, part)], gbuf.at[j, d], own_sem.at[j])
+
+    def out_copy(k):
+        start = pl.multiple_of(peers[k] * cols + s * part, part)
+        return pltpu.make_async_copy(grads_ref.at[:, pl.ds(start, part)], gsend.at[k], out_sem.at[k])
+
+    act_copy = pltpu.make_async_copy(acts_ref, abuf.at[d], act_sem)
+    abasis_copy = pltpu.make_async_copy(abasis_ref, abasis, ab_sem)
+    gbasis_copy = pltpu.make_async_copy(gbasis_ref, gbasis, gb_sem)
+
+    def val_copy(c, slot):
+        at = pl.multiple_of(c * chunk, chunk)
+        return pltpu.make_async_copy(val_ref.at[:, pl.ds(at, chunk), :], val_buf.at[slot], val_sem.at[slot])
+
+    def corr_copy(c, slot):
+        at = pl.multiple_of(c * chunk, chunk)
+        return pltpu.make_async_copy(corr_ref.at[pl.ds(at, chunk), :], corr_buf.at[slot], corr_sem.at[slot])
+
+    for k in range(n_dp - 1):
+        out_copy(k).start()
+    act_copy.start()
+    for j in range(n_shard):
+        own_copy(j).start()
+    gbasis_copy.start()
+    abasis_copy.start()
+
+    @pl.loop(0, slots)
+    def _(c):
+        corr_copy(c, c).start()
+        val_copy(c, c).start()
+
+    barrier = pltpu.get_barrier_semaphore()
+    for p in peers:
+        pl.semaphore_signal(barrier, inc=1, device_id={"dp": p}, device_id_type=MESH)
+    for p in (other_core, other_chip, across):
+        pl.semaphore_signal(barrier, inc=1, device_id={"shard": p}, device_id_type=MESH)
+
+    row_at = lax.broadcasted_iota(jnp.int32, (tok, part), 0)
+    limit = jnp.zeros((tok, part), jnp.int32)
+    for q in range(n_seq):
+        limit = jnp.where(row_at // seq_len == q, len_ref[q], limit)
+    keep = lax.rem(row_at, seq_len) < limit
+
+    def masked(x):
+        return jnp.where(keep, x.astype(jnp.float32), 0.0).astype(jnp.bfloat16)
+
+    for k in range(n_dp - 1):
+        out_copy(k).wait()
+        gsend[k] = masked(gsend[k])
+
+    pl.semaphore_wait(barrier, n_dp - 1 + 3)
+
+    def grad_send(k):
+        return pltpu.make_async_remote_copy(
+            gsend.at[k], gbuf.at[s, d], gsend_sem.at[k], grecv_sem.at[s, d],
+            device_id={"dp": peers[k]}, device_id_type=MESH)
+
+    def grad_arrival(j, p):
+        return pltpu.make_async_remote_copy(
+            gsend.at[0], gbuf.at[j, p], gsend_sem.at[0], grecv_sem.at[j, p],
+            device_id={"dp": peers[0]}, device_id_type=MESH)
+
+    order = [0, n_dp - 2] + list(range(1, n_dp - 2)) if n_dp > 2 else list(range(n_dp - 1))
+    for k in order:
+        grad_send(k).start()
+
+    act_copy.wait()
+    for j in range(abuf.shape[2] // part):
+        abuf[d, :, j * part:(j + 1) * part] = masked(abuf[d, :, j * part:(j + 1) * part])
+
+    def act_send(k):
+        return pltpu.make_async_remote_copy(
+            abuf.at[d], abuf.at[d], asend_sem.at[k], arecv_sem.at[d],
+            device_id={"dp": peers[k]}, device_id_type=MESH)
+
+    def act_arrival(p):
+        return pltpu.make_async_remote_copy(
+            abuf.at[d], abuf.at[p], asend_sem.at[0], arecv_sem.at[p],
+            device_id={"dp": peers[0]}, device_id_type=MESH)
+
+    for k in order:
+        act_send(k).start()
+
+    for j in range(n_shard):
+        own_copy(j).wait()
+        gbuf[j, d] = masked(gbuf[j, d])
+
+    def pass_on(k, j, sems, target):
+        p = peers[k]
+        return pltpu.make_async_remote_copy(
+            gbuf.at[j, p], gbuf.at[j, p], sems.at[k], grecv_sem.at[j, p],
+            device_id={"shard": target}, device_id_type=MESH)
+
+    for k in order:
+        grad_arrival(s, peers[k]).wait_recv()
+        pass_on(k, s, fx_sem, other_chip).start()
+        pass_on(k, s, fc_sem, other_core).start()
+
+    gbasis_copy.wait()
+
+    def turn_part(j):
+        x = gbuf[j].reshape(tokens, part)
+        for b in range(part_blocks):
+            y = jnp.dot(x[:, b * blk:(b + 1) * blk], gbasis[j * part_blocks + b],
+                        preferred_element_type=jnp.float32)
+            at = pl.multiple_of((j * part_blocks + b) * blk, blk)
+            g_t[pl.ds(at, blk), :] = y.T.astype(jnp.bfloat16)
+
+    turn_part(s)
+    for k in order:
+        grad_arrival(other_chip, peers[k]).wait_recv()
+        pass_on(k, other_chip, fr_sem, other_core).start()
+    turn_part(other_chip)
+    for k in order:
+        grad_arrival(other_core, peers[k]).wait_recv()
+    turn_part(other_core)
+    for k in order:
+        grad_arrival(across, peers[k]).wait_recv()
+    turn_part(across)
+
+    abasis_copy.wait()
+    for k in order:
+        act_arrival(peers[k]).wait_recv()
+    for b in range(a_blocks):
+        x = abuf[:, :, b * blk:(b + 1) * blk].reshape(tokens, blk)
+        y = jnp.dot(x, abasis[b], preferred_element_type=jnp.float32)
+        a_t[b * blk:(b + 1) * blk, :] = y.astype(jnp.bfloat16).astype(jnp.float32).T
+
+    acc[...] = jnp.zeros_like(acc)
+
+    @pl.loop(0, chunks)
+    def _(c):
+        slot = lax.rem(c, slots)
+        corr_copy(c, slot).wait()
+        val_copy(c, slot).wait()
+
+        def column_step(j, sums):
+            at = pl.multiple_of(j * kstep, kstep)
+            inverse = 1.0 / (corr_buf[slot, :, pl.ds(at, kstep)].astype(jnp.float32) + damping)
+            right = g_t[pl.ds(at, kstep), :]
+            out = []
+            for q in range(queries):
+                pre = (val_buf[slot, q, :, pl.ds(at, kstep)].astype(jnp.float32) * inverse).astype(jnp.bfloat16)
+                out.append(sums[q] + jnp.dot(pre, right, preferred_element_type=jnp.float32))
+            return tuple(out)
+
+        zero = jnp.zeros((chunk, tokens), jnp.float32)
+        sums = lax.fori_loop(0, cols // kstep, column_step, (zero,) * queries)
+        weight = a_t[pl.ds(pl.multiple_of(c * chunk, chunk), chunk), :]
+        for q in range(queries):
+            acc[q] += jnp.sum((sums[q] * weight).reshape(chunk // 8, 8, tokens), axis=0)
+
+        @pl.when(c + slots < chunks)
+        def _():
+            corr_copy(c + slots, slot).start()
+            val_copy(c + slots, slot).start()
+
+    for q in range(queries):
+        red_dp[d, q:q + 1, :] = jnp.sum(acc[q], axis=0, keepdims=True)
+    red_dp[d, queries:, :] = jnp.zeros((8 - queries, tokens), jnp.float32)
+
+    def dp_send(k):
+        return pltpu.make_async_remote_copy(
+            red_dp.at[d], red_dp.at[d], rds_sem.at[k], rdr_sem.at[d],
+            device_id={"dp": peers[k]}, device_id_type=MESH)
+
+    def dp_arrival(k):
+        return pltpu.make_async_remote_copy(
+            red_dp.at[d], red_dp.at[peers[k]], rds_sem.at[k], rdr_sem.at[peers[k]],
+            device_id={"dp": peers[k]}, device_id_type=MESH)
+
+    for k in range(n_dp - 1):
+        dp_send(k).start()
+
+    a_rows = blk // n_dp
+    lane = lax.broadcasted_iota(jnp.int32, (a_rows, tokens), 1)
+    for b in range(a_blocks):
+        x = abuf[:, :, b * blk:(b + 1) * blk].reshape(tokens, blk)
+        turn[b] = x.astype(jnp.float32).T
+        left = turn[b, pl.ds(pl.multiple_of(d * a_rows, a_rows), a_rows), :]
+        total = jnp.zeros((a_rows, blk), jnp.float32)
+        for r in range(n_dp):
+            run = jnp.where(lane // tok == r, left, 0.0).astype(jnp.bfloat16)
+            total += jnp.dot(run, x, preferred_element_type=jnp.float32).astype(jnp.bfloat16).astype(jnp.float32)
+        acov_ref[b] = total / tokens
+
+    for k in range(n_dp - 1):
+        dp_arrival(k).wait_recv()
+    total = red_dp[0]
+    for p in range(1, n_dp):
+        total += red_dp[p]
+    red_sh[s] = total
+
+    others = (other_core, other_chip, across)
+
+    def sh_send(k):
+        return pltpu.make_async_remote_copy(
+            red_sh.at[s], red_sh.at[s], rss_sem.at[k], rsr_sem.at[s],
+            device_id={"shard": others[k]}, device_id_type=MESH)
+
+    def sh_arrival(k):
+        return pltpu.make_async_remote_copy(
+            red_sh.at[s], red_sh.at[others[k]], rss_sem.at[k], rsr_sem.at[others[k]],
+            device_id={"shard": others[k]}, device_id_type=MESH)
+
+    for k in range(3):
+        sh_send(k).start()
+
+    g_rows = blk // n_shard
+    for j in range(n_shard):
+        for b in range(part_blocks):
+            at = b % turn.shape[0]
+            x = gbuf[j, :, :, b * blk:(b + 1) * blk].reshape(tokens, blk)
+            turn[at] = x.astype(jnp.float32).T
+            left = turn[at, pl.ds(pl.multiple_of(s * g_rows, g_rows), g_rows), :].astype(jnp.bfloat16)
+            gcov_ref[j * part_blocks + b] = jnp.dot(left, x, preferred_element_type=jnp.float32) / tokens
+
+    for k in range(3):
+        sh_arrival(k).wait_recv()
+    total = red_sh[0]
+    for p in range(1, n_shard):
+        total += red_sh[p]
+    lane = lax.broadcasted_iota(jnp.int32, (8, tokens), 1)
+    row = lax.broadcasted_iota(jnp.int32, (8, tokens), 0)
+    for q in range(n_seq):
+        one = jnp.sum(jnp.where(lane // seq_len == d * n_seq + q, total, 0.0), axis=1, keepdims=True)
+        line = jnp.sum(jnp.where(lane == row, one, 0.0), axis=0, keepdims=True)
+        scores_ref[q:q + 1, :] = line[:, :queries]
+
+    for k in range(n_dp - 1):
+        grad_send(k).wait_send()
+        act_send(k).wait_send()
+        pass_on(k, s, fx_sem, other_chip).wait_send()
+        pass_on(k, s, fc_sem, other_core).wait_send()
+        pass_on(k, other_chip, fr_sem, other_core).wait_send()
+        dp_send(k).wait_send()
+    for k in range(3):
+        sh_send(k).wait_send()
+
+
+def fits(n_dp, n_shard, acts, lengths, act_basis, grad_basis, val_grads):
+    tok = acts.shape[0]
+    blk = act_basis.shape[1]
+    queries, rows, cols = val_grads.shape
+    return (
+        n_shard == 4 and tok * n_dp == 128 and tok % 16 == 0 and queries <= 7
+        and tok % lengths.shape[0] == 0 and blk % 128 == 0
+        and blk % (16 * n_dp) == 0 and blk % (16 * n_shard) == 0
+        and cols % (blk * n_shard) == 0 and rows % (cols // n_shard) == 0 and rows % 64 == 0
+    )
+
+
+def local(acts, grads, lengths, act_basis, grad_basis, correction, val_grads):
+    n_dp = lax.axis_size("dp")
+    n_shard = lax.axis_size("shard")
+    if not fits(n_dp, n_shard, acts, lengths, act_basis, grad_basis, val_grads):
+        return local_plain(acts, grads, lengths, act_basis, grad_basis, correction, val_grads)
+    tok = acts.shape[0]
+    tokens = tok * n_dp
+    blk = act_basis.shape[1]
+    a_blocks, g_blocks = act_basis.shape[0], grad_basis.shape[0]
+    queries, rows, cols = val_grads.shape
+    part = cols // n_shard
+    chunk = 64
+    slots = min(rows // chunk, STREAM_BYTES // ((queries + 1) * chunk * cols * 2))
+    kstep = min(512, cols)
+    dma = pltpu.SemaphoreType.DMA
+    bf16, f32 = jnp.bfloat16, jnp.float32
+    anywhere = pl.BlockSpec(memory_space=pl.ANY)
+    vmem = pl.BlockSpec(memory_space=pltpu.VMEM)
+    return pl.pallas_call(
+        functools.partial(kernel, n_dp, n_shard, chunk, slots, kstep),
+        out_shape=(
+            jax.ShapeDtypeStruct((lengths.shape[0], queries), f32),
+            jax.ShapeDtypeStruct((a_blocks, blk // n_dp, blk), f32),
+            jax.ShapeDtypeStruct((g_blocks, blk // n_shard, blk), f32),
+        ),
+        in_specs=[pl.BlockSpec(memory_space=pltpu.SMEM)] + [anywhere] * 6,
+        out_specs=(vmem, vmem, vmem),
+        scratch_shapes=[
+            pltpu.VMEM((n_shard, n_dp, tok, part), bf16),
+            pltpu.VMEM((n_dp - 1, tok, part), bf16),
+            pltpu.VMEM((n_dp, tok, rows), bf16),
+            pltpu.VMEM((a_blocks, blk, blk), bf16),
+            pltpu.VMEM((g_blocks, blk, blk), bf16),
+            pltpu.VMEM((cols, tokens), bf16),
+            pltpu.VMEM((rows, tokens), f32),
+            pltpu.VMEM((max(a_blocks, 2), blk, tokens), f32),
+            pltpu.VMEM((slots, queries, chunk, cols), bf16),
+            pltpu.VMEM((slots, chunk, cols), bf16),
+            pltpu.VMEM((queries, 8, tokens), f32),
+            pltpu.VMEM((n_dp, 8, tokens), f32),
+            pltpu.VMEM((n_shard, 8, tokens), f32),
+            dma((n_shard,)), dma((n_dp - 1,)), dma(()), dma(()), dma(()), dma((slots,)), dma((slots,)),
+            dma((n_dp - 1,)), dma((n_shard, n_dp)), dma((n_dp - 1,)), dma((n_dp,)),
+            dma((n_dp - 1,)), dma((n_dp - 1,)), dma((n_dp - 1,)),
+            dma((n_dp - 1,)), dma((n_dp,)), dma((3,)), dma((n_shard,)),
+        ],
+        compiler_params=pltpu.CompilerParams(
+            collective_id=0, has_side_effects=True, vmem_limit_bytes=VMEM_LIMIT
+        ),
+        name="scores_and_covariances",
+    )(lengths, acts, grads, act_basis, grad_basis, correction, val_grads)
+
+
 def solution(mesh):
     in_specs = (
         P(("groups", "dp"), "shard"),

time: 146 us -> 72.2 us (0.49)
  blocking collectives: 68.2 us -> 0 us
  Pallas kernels: 0 us -> 66.2 us
  matrix products: 33.2 us -> 0 us
  other arithmetic: 16.3 us -> 0 us
  between operations: 14.1 us -> 0.64 us
  starting transfers between devices: 6.32 us -> 0 us
  local copies, waits for them, and re-layouts: 7.77 us -> 5.16 us
    pallas_call x0 -> x1, Pallas kernels: none -> 66.2 us  [local(): pl.pallas_call(functools.partial(kernel, n_dp, n_shard, chunk, slots, kst...]
    all_gather x1 -> x0, blocking collectives: 38.5 us -> none  [local(): arrived = lax.all_gather(act_turned, 'dp', axis=0, tiled=True)]
    dot_general x5 -> x0, matrix products: 33.2 us -> none  [the longest x1 27.8 us: local(): jnp.einsum('tj,qij->tqi', grad_turned, precond, preferred_element_type=jn...]
    psum x1 -> x0, blocking collectives: 29.8 us -> none  [local(): everything = lax.psum(seq_scores, ('dp', 'shard'))]
    add x1 -> x0, other arithmetic: 11.5 us -> none  [local(): correction.astype(jnp.float32) + damping]
    all_to_all x1 -> x0, starting transfers between devices: 6.32 us -> none  [local(): lax.all_to_all(grad_masked, 'dp', split_axis=1, concat_axis=0, tiled=True)]
    convert_element_type x2 -> x0, local copies, waits for them, and re-layouts: 2.29 us -> none  [rotate_blocks(): rotated.reshape(row_count, block_count * block_width).astype(jnp.bfloat16)]
    mul x2 -> x0, other arithmetic: 2.28 us -> none  [the longest x1 1.36 us: local(): grad_masked = grads * token_keep]
  transfers between devices with their start and end apart: 2 -> 0, of which waited for: 0 -> 0; matrix products, arithmetic and copies ran while one was open for 12% -> 0% of each run, Pallas kernels for 0% -> 0%
where the time goes in v1:
time: 72.2 us; the launch traced here: 72 us
  Pallas kernels  66.2 us (92%)
  local copies, waits for them, and re-layouts  5.16 us (7%)
    pallas_call x1, Pallas kernels, local(): pl.pallas_call(functools.partial(kernel, n_dp, n_shard, chunk, slots, kst...  66.2 us
    unnamed x3, local copies, waits for them, and re-layouts  5.16 us

profile of v1, /device:TPU:0, one launch (start us, length us, event | category | flops | bytes accessed | tf_op | source)
XLA Modules:
  0.0 72.0 jit_solution(6402152226007875870)
XLA Ops:
  0.6 66.2 %scores_and_covariances.1 = (f32[2,6]{1,0:T(2,128)}, f32[4,64,256]{2,1,0:T(8,128)}, f32[16,64,256]{2,1,0:T(8,128)}) custom-call(s32[2]{0:T(128)} %len_ref.1, bf16[32,1024]{1,0:T(8,128)(2,1)} %acts_ref.1, bf16[32,16384]{1,0:T(8,128)(2,1)} %grads_ref.1, bf16[4,256,256]{2,1,0:T(8,128)(2,1)} %abasis_ref.1, bf16[16,256,256]{2,1,0:T(8,128)(2,1)} %gbasis_ref.1, ...), custom_call_target="tpu_custom_call" | custom-call | tf_op jit(solution)/shard_map/scores_and_covariances/pallas_call | solution.py:377
  66.8 1.2 %copy.13 = f32[2,6]{1,0:T(2,128)} copy(f32[2,6]{1,0:T(2,128)} %get-tuple-element.6) | data formatting | bytes 96
  68.0 1.7 %copy.14 = f32[4,64,256]{2,1,0:T(8,128)} copy(f32[4,64,256]{2,1,0:T(8,128)} %get-tuple-element.7) | data formatting | bytes 524288
  69.7 2.3 %copy.15 = f32[16,64,256]{2,1,0:T(8,128)} copy(f32[16,64,256]{2,1,0:T(8,128)} %get-tuple-element.8) | data formatting | bytes 2097152

commit v2 on v1

--- a/solution.py
+++ b/solution.py
@@ -122,6 +122,12 @@
         at = pl.multiple_of(c * chunk, chunk)
         return pltpu.make_async_copy(corr_ref.at[pl.ds(at, chunk), :], corr_buf.at[slot], corr_sem.at[slot])
 
+    barrier = pltpu.get_barrier_semaphore()
+    for p in peers:
+        pl.semaphore_signal(barrier, inc=1, device_id={"dp": p}, device_id_type=MESH)
+    for p in (other_core, other_chip, across):
+        pl.semaphore_signal(barrier, inc=1, device_id={"shard": p}, device_id_type=MESH)
+
     for k in range(n_dp - 1):
         out_copy(k).start()
     act_copy.start()
@@ -135,12 +141,6 @@
         corr_copy(c, c).start()
         val_copy(c, c).start()
 
-    barrier = pltpu.get_barrier_semaphore()
-    for p in peers:
-        pl.semaphore_signal(barrier, inc=1, device_id={"dp": p}, device_id_type=MESH)
-    for p in (other_core, other_chip, across):
-        pl.semaphore_signal(barrier, inc=1, device_id={"shard": p}, device_id_type=MESH)
-
     row_at = lax.broadcasted_iota(jnp.int32, (tok, part), 0)
     limit = jnp.zeros((tok, part), jnp.int32)
     for q in range(n_seq):
@@ -241,20 +241,21 @@
         val_copy(c, slot).wait()
 
         def column_step(j, sums):
-            at = pl.multiple_of(j * kstep, kstep)
+            at = j * kstep
             inverse = 1.0 / (corr_buf[slot, :, pl.ds(at, kstep)].astype(jnp.float32) + damping)
             right = g_t[pl.ds(at, kstep), :]
-            out = []
-            for q in range(queries):
-                pre = (val_buf[slot, q, :, pl.ds(at, kstep)].astype(jnp.float32) * inverse).astype(jnp.bfloat16)
-                out.append(sums[q] + jnp.dot(pre, right, preferred_element_type=jnp.float32))
-            return tuple(out)
-
-        zero = jnp.zeros((chunk, tokens), jnp.float32)
-        sums = lax.fori_loop(0, cols // kstep, column_step, (zero,) * queries)
+            pre = [
+                (val_buf[slot, q, :, pl.ds(at, kstep)].astype(jnp.float32) * inverse).astype(jnp.bfloat16)
+                for q in range(queries)
+            ]
+            return sums + jnp.dot(jnp.concatenate(pre, axis=0), right, preferred_element_type=jnp.float32)
+
+        sums = jnp.zeros((queries * chunk, tokens), jnp.float32)
+        for j in range(cols // kstep):
+            sums = column_step(j, sums)
         weight = a_t[pl.ds(pl.multiple_of(c * chunk, chunk), chunk), :]
         for q in range(queries):
-            acc[q] += jnp.sum((sums[q] * weight).reshape(chunk // 8, 8, tokens), axis=0)
+            acc[q] += jnp.sum((sums[q * chunk:(q + 1) * chunk] * weight).reshape(chunk // 8, 8, tokens), axis=0)
 
         @pl.when(c + slots < chunks)
         def _():
@@ -344,6 +345,12 @@
         sh_send(k).wait_send()
 
 
+def hand_on(a, b, c, x, y, z):
+    x[...] = a[...]
+    y[...] = b[...]
+    z[...] = c[...]
+
+
 def fits(n_dp, n_shard, acts, lengths, act_basis, grad_basis, val_grads):
     tok = acts.shape[0]
     blk = act_basis.shape[1]
@@ -352,7 +359,7 @@
         n_shard == 4 and tok * n_dp == 128 and tok % 16 == 0 and queries <= 7
         and tok % lengths.shape[0] == 0 and blk % 128 == 0
         and blk % (16 * n_dp) == 0 and blk % (16 * n_shard) == 0
-        and cols % (blk * n_shard) == 0 and rows % (cols // n_shard) == 0 and rows % 64 == 0
+        and cols % (blk * n_shard) == 0 and rows % (cols // n_shard) == 0 and rows % 128 == 0
     )
 
 
@@ -367,14 +374,14 @@
     a_blocks, g_blocks = act_basis.shape[0], grad_basis.shape[0]
     queries, rows, cols = val_grads.shape
     part = cols // n_shard
-    chunk = 64
+    chunk = 128
     slots = min(rows // chunk, STREAM_BYTES // ((queries + 1) * chunk * cols * 2))
-    kstep = min(512, cols)
+    kstep = min(1024, cols)
     dma = pltpu.SemaphoreType.DMA
     bf16, f32 = jnp.bfloat16, jnp.float32
     anywhere = pl.BlockSpec(memory_space=pl.ANY)
     vmem = pl.BlockSpec(memory_space=pltpu.VMEM)
-    return pl.pallas_call(
+    results = pl.pallas_call(
         functools.partial(kernel, n_dp, n_shard, chunk, slots, kstep),
         out_shape=(
             jax.ShapeDtypeStruct((lengths.shape[0], queries), f32),
@@ -407,6 +414,13 @@
         ),
         name="scores_and_covariances",
     )(lengths, acts, grads, act_basis, grad_basis, correction, val_grads)
+    return pl.pallas_call(
+        hand_on,
+        out_shape=tuple(jax.ShapeDtypeStruct(r.shape, r.dtype) for r in results),
+        in_specs=[vmem] * 3,
+        out_specs=(vmem,) * 3,
+        name="hand_on_results",
+    )(*results)
 
 
 def solution(mesh):

time: 72.2 us -> 46.9 us (0.65)
  Pallas kernels: 66.2 us -> 46.1 us
  local copies, waits for them, and re-layouts: 5.16 us -> 0 us
    pallas_call x1, Pallas kernels: 66.2 us -> 43.7 us  [local(): pl.pallas_call(functools.partial(kernel, n_dp, n_shard, chunk, slots, kst...]
    unnamed x3 -> x0, local copies, waits for them, and re-layouts: 5.16 us -> none
    pallas_call x0 -> x1, Pallas kernels: none -> 2.4 us  [local(): pl.pallas_call(hand_on, out_shape=tuple((jax.ShapeDtypeStruct(r.shape, r....]
where the time goes in v2:
time: 46.9 us; the launch traced here: 46.7 us
  Pallas kernels  46.1 us (98%)
  between operations  0.64 us (1%)
    pallas_call x1, Pallas kernels, local(): pl.pallas_call(functools.partial(kernel, n_dp, n_shard, chunk, slots, kst...  43.7 us
    pallas_call x1, Pallas kernels, local(): pl.pallas_call(hand_on, out_shape=tuple((jax.ShapeDtypeStruct(r.shape, r....  2.4 us

profile of v2, /device:TPU:0, one launch (start us, length us, event | category | flops | bytes accessed | tf_op | source)
XLA Modules:
  0.0 46.7 jit_solution(1798232980013525621)
XLA Ops:
  0.6 43.7 %scores_and_covariances.1 = (f32[2,6]{1,0:T(2,128)}, f32[4,64,256]{2,1,0:T(8,128)}, f32[16,64,256]{2,1,0:T(8,128)}) custom-call(s32[2]{0:T(128)} %len_ref.1, bf16[32,1024]{1,0:T(8,128)(2,1)} %acts_ref.1, bf16[32,16384]{1,0:T(8,128)(2,1)} %grads_ref.1, bf16[4,256,256]{2,1,0:T(8,128)(2,1)} %abasis_ref.1, bf16[16,256,256]{2,1,0:T(8,128)(2,1)} %gbasis_ref.1, ...), custom_call_target="tpu_custom_call" | custom-call | tf_op jit(solution)/shard_map/scores_and_covariances/pallas_call | solution.py:384
  44.3 2.4 %hand_on_results.1 = (f32[2,6]{1,0:T(2,128)}, f32[4,64,256]{2,1,0:T(8,128)}, f32[16,64,256]{2,1,0:T(8,128)}) custom-call(f32[2,6]{1,0:T(2,128)} %get-tuple-element.6.a, f32[4,64,256]{2,1,0:T(8,128)} %get-tuple-element.7.b, f32[16,64,256]{2,1,0:T(8,128)} %get-tuple-element.8.c), custom_call_target="tpu_custom_call" | custom-call | tf_op jit(solution)/shard_map/hand_on_results/pallas_call | solution.py:417
